TPU v7x, 32 devices: a whole 2x2x4 slice. The times are simulated.
32 devices in a mesh: grp: 4 (over y, x), gx: 4 (over z), gy: 2 (over core).
Axes of the slice: x: 2, y: 2, z: 4, core: 2. Of those that a mesh axis runs over, the one named last changes fastest.
Arguments:
- fwd_now: float32 [3, 16, 16, 128], P(None, 'gx', 'gy'), may hold values from -6 to 6
- fwd_prev: float32 [3, 16, 16, 128], P(None, 'gx', 'gy'), may hold values from -6 to 6
- adj_now: float32 [16, 3, 16, 16, 128], P('grp', None, 'gx', 'gy'), may hold values from -6 to 6
- adj_prev: float32 [16, 3, 16, 16, 128], P('grp', None, 'gx', 'gy'), may hold values from -6 to 6
- lame_first: float32 [16, 16, 128], P('gx', 'gy'), may hold values from 0.5 to 2
- shear_mod: float32 [16, 16, 128], P('gx', 'gy'), may hold values from 0.3 to 1.2
- buoyancy: float32 [16, 16, 128], P('gx', 'gy'), may hold values from 0.5 to 1
- master_cell: int32 [1], replicated, may hold values from 0 to 32767
- master_lag: int32 [1], replicated, may hold values from 0 to 254
- master_trace: float32 [256, 3], replicated, may hold values from -96 to 96
- receiver_cell: int32 [16], P('grp'), may hold values from 0 to 32767
- receiver_lag: int32 [16], P('grp'), may hold values from 0 to 254
- receiver_trace: float32 [16, 256, 3], P('grp'), may hold values from -96 to 96
Outputs:
- adj_final: float32 [16, 3, 16, 16, 128], P('grp', None, 'gx', 'gy')
- kernels: float32 [2, 16, 16, 128], P(None, 'gx', 'gy', 'grp')
Inputs may be any that keep to these rules, and one draw needn't show every extreme that they name: `receiver_cell`: cell index in the whole grid, numbered (x * 16 + y) * 128 + z. `master_cell`: cell index in the whole grid, numbered (x * 16 + y) * 128 + z.
All inputs are finite; a program needn't handle non-finite values.
Results may differ from a plain program's by a relative error of at most 0.00011.
Values sent between devices are 32-bit elements; how exact they have to be, the bound alone decides.
A program may use at most 64 MiB of HBM per device.

v0:
```python
import jax
import jax.numpy as jnp
from jax import lax
from jax.sharding import PartitionSpec as P

STEPS = 2


time_step_sq = 0.0625


def with_halo(cells, sides, width):
    for axis, dim in sides:
        count = lax.axis_size(axis)
        ends = count - 1
        head = lax.slice_in_dim(cells, 0, width, axis=dim)
        tail = lax.slice_in_dim(cells, cells.shape[dim] - width, cells.shape[dim], axis=dim)
        cells = jnp.concatenate(
            [
                lax.ppermute(tail, axis, [(i, (i + 1) % count) for i in range(ends)]),
                cells,
                lax.ppermute(head, axis, [((i + 1) % count, i) for i in range(ends)]),
            ],
            axis=dim,
        )
    return cells


def passed_along(value, axis, by):
    size = lax.axis_size(axis)
    pairs = [(i, i + by) for i in range(size) if 0 <= i + by < size]
    return lax.ppermute(value, axis, pairs)


def backward_diff(stress, axis):
    upper = stress[:, 1:, 1:, 1:]
    if axis == 1:
        lower = stress[:, :-1, 1:, 1:]
    elif axis == 2:
        lower = stress[:, 1:, :-1, 1:]
    else:
        lower = stress[:, 1:, 1:, :-1]
    return upper - lower


def stencil(padded, lame_pad, shear_pad):
    span_x = padded.shape[2] - 2
    span_y = padded.shape[3] - 2
    span_z = padded.shape[4] - 2
    anchor = padded[:, :, : span_x + 1, : span_y + 1, : span_z + 1]
    grad_x = padded[:, :, 1:, : span_y + 1, : span_z + 1] - anchor
    grad_y = padded[:, :, : span_x + 1, 1:, : span_z + 1] - anchor
    grad_z = padded[:, :, : span_x + 1, : span_y + 1, 1:] - anchor
    strain_xx = grad_x[:, 0]
    strain_yy = grad_y[:, 1]
    strain_zz = grad_z[:, 2]
    strain_xy = 0.5 * (grad_y[:, 0] + grad_x[:, 1])
    strain_xz = 0.5 * (grad_z[:, 0] + grad_x[:, 2])
    strain_yz = 0.5 * (grad_z[:, 1] + grad_y[:, 2])
    lame = lame_pad[: span_x + 1, : span_y + 1, : span_z + 1]
    shear = shear_pad[: span_x + 1, : span_y + 1, : span_z + 1]
    dilation = strain_xx + strain_yy + strain_zz
    stress_xx = lame * dilation + 2.0 * shear * strain_xx
    stress_yy = lame * dilation + 2.0 * shear * strain_yy
    stress_zz = lame * dilation + 2.0 * shear * strain_zz
    stress_xy = 2.0 * shear * strain_xy
    stress_xz = 2.0 * shear * strain_xz
    stress_yz = 2.0 * shear * strain_yz
    force_x = (
        backward_diff(stress_xx, 1) + backward_diff(stress_xy, 2) + backward_diff(stress_xz, 3)
    )
    force_y = (
        backward_diff(stress_xy, 1) + backward_diff(stress_yy, 2) + backward_diff(stress_yz, 3)
    )
    force_z = (
        backward_diff(stress_xz, 1) + backward_diff(stress_yz, 2) + backward_diff(stress_zz, 3)
    )
    force = jnp.stack([force_x, force_y, force_z], axis=1)
    strain = jnp.stack([strain_xx, strain_yy, strain_zz, strain_xy, strain_xz, strain_yz], axis=1)
    return (force, strain[:, :, 1:, 1:, 1:])


def faces(fields):
    count = fields.shape[0]
    flat = fields.reshape((count * 3,) + fields.shape[2:])
    grown = with_halo(flat, (("gx", 1), ("gy", 2)), 1)
    grown = jnp.pad(grown, ((0, 0), (0, 0), (0, 0), (1, 1)))
    return grown.reshape((count, 3) + grown.shape[1:])


def lower_rims(moduli):
    pairs, cells_x, cells_y, depth = moduli.shape
    from_x = passed_along(moduli[:, cells_x - 1 :], "gx", 1)
    from_y = passed_along(moduli[:, :, cells_y - 1 :], "gy", 1)
    corner = jnp.zeros((pairs, 1, 1, depth), jnp.float32)
    top_row = jnp.concatenate([corner, from_y], axis=1)
    rest = jnp.concatenate([from_x, moduli], axis=1)
    grown = jnp.concatenate([top_row, rest], axis=2)
    return jnp.pad(grown, ((0, 0), (0, 1), (0, 1), (1, 1)))


def locate(cells, start_x, start_y, start_z, width_y, depth, span_x, span_y, span_z):
    coord_x = cells // (width_y * depth) - start_x
    coord_y = cells // depth % width_y - start_y
    coord_z = cells % depth - start_z
    index_x = lax.broadcasted_iota(jnp.int32, (1, span_x, 1, 1), 1)
    index_y = lax.broadcasted_iota(jnp.int32, (1, 1, span_y, 1), 2)
    index_z = lax.broadcasted_iota(jnp.int32, (1, 1, 1, span_z), 3)
    found = (
        (index_x == coord_x[:, None, None, None])
        & (index_y == coord_y[:, None, None, None])
        & (index_z == coord_z[:, None, None, None])
    )
    return found.astype(jnp.float32)


def pick(trace, lags):
    positions = lax.broadcasted_iota(jnp.int32, (1, trace.shape[1]), 1)
    chosen = positions == lags[:, None]
    return jnp.sum(jnp.where(chosen[:, :, None], trace, 0.0), axis=1)


def advance(current, earlier, force, amplitudes, masks, buoyancy):
    source = amplitudes[:, :, None, None, None] * masks[:, None]
    return 2.0 * current - earlier + time_step_sq * buoyancy * (force + source)


def correlate(master, strains, totals):
    weights = jnp.array([1.0, 1.0, 1.0, 2.0, 2.0, 2.0], jnp.float32)[:, None, None, None]
    summed = jnp.sum(strains, axis=0)
    dilation_term = (master[0] + master[1] + master[2]) * (summed[0] + summed[1] + summed[2])
    shear_term = 2.0 * jnp.sum(weights * master * summed, axis=0)
    return totals + jnp.stack([dilation_term, shear_term])


def local(
    fwd_now,
    fwd_prev,
    adj_now,
    adj_prev,
    lame_first,
    shear_mod,
    buoyancy,
    master_cell,
    master_lag,
    master_trace,
    receiver_cell,
    receiver_lag,
    receiver_trace,
):
    cells_x, cells_y, depth = lame_first.shape
    groups = lax.axis_size("grp")
    receivers = adj_now.shape[0]
    width_y = cells_y * lax.axis_size("gy")
    start_x = lax.axis_index("gx") * cells_x
    start_y = lax.axis_index("gy") * cells_y
    moduli = lower_rims(jnp.stack([lame_first, shear_mod]))
    lame_pad = moduli[0]
    shear_pad = moduli[1]
    receiver_masks = locate(
        receiver_cell, start_x, start_y, 0, width_y, depth, cells_x, cells_y, depth
    )
    receiver_amps = [pick(receiver_trace, receiver_lag + instant) for instant in range(STEPS)]
    master_amps = [pick(master_trace[None], master_lag + instant) for instant in range(STEPS)]
    totals = jnp.zeros((2, cells_x, cells_y, depth), jnp.float32)
    share = depth // groups
    z_start = lax.axis_index("grp") * share
    master_now = lax.dynamic_slice_in_dim(fwd_now, z_start, share, 3)
    master_prev = lax.dynamic_slice_in_dim(fwd_prev, z_start, share, 3)
    lame_share = lax.dynamic_slice_in_dim(lame_pad, z_start, share + 2, 2)
    shear_share = lax.dynamic_slice_in_dim(shear_pad, z_start, share + 2, 2)
    buoyancy_share = lax.dynamic_slice_in_dim(buoyancy, z_start, share, 2)
    master_mask = locate(
        master_cell, start_x, start_y, z_start, width_y, depth, cells_x, cells_y, share
    )
    adjoint = adj_now
    adjoint_prev = adj_prev
    for instant in range(STEPS):
        grown = with_halo(master_now, (("grp", 3), ("gx", 1), ("gy", 2)), 1)
        master_force, master_strain = stencil(grown[None], lame_share, shear_share)
        master_whole = lax.all_gather(master_strain[0], "grp", axis=3, tiled=True)
        if instant + 1 < STEPS:
            master_next = advance(
                master_now[None],
                master_prev[None],
                master_force,
                master_amps[instant],
                master_mask,
                buoyancy_share,
            )[0]
            master_prev, master_now = (master_now, master_next)
        padded = faces(adjoint)
        force, strain = stencil(padded, lame_pad, shear_pad)
        totals = correlate(master_whole, strain, totals)
        adjoint_next = advance(
            adjoint, adjoint_prev, force, receiver_amps[instant], receiver_masks, buoyancy
        )
        adjoint_prev, adjoint = (adjoint, adjoint_next)
    scale_out = 1.0 / (STEPS * receivers * groups)
    kernels = lax.psum_scatter(totals * scale_out, "grp", scatter_dimension=3, tiled=True)
    return (adjoint, kernels)


def solution(mesh):
    in_specs = (
        P(None, "gx", "gy", None),
        P(None, "gx", "gy", None),
        P("grp", None, "gx", "gy", None),
        P("grp", None, "gx", "gy", None),
        P("gx", "gy", None),
        P("gx", "gy", None),
        P("gx", "gy", None),
        P(),
        P(),
        P(),
        P("grp"),
        P("grp"),
        P("grp", None, None),
    )
    out_specs = (P("grp", None, "gx", "gy", None), P(None, "gx", "gy", "grp"))
    return jax.shard_map(local, mesh=mesh, in_specs=in_specs, out_specs=out_specs, check_vma=False)
```

profile of v0, /device:TPU:0, one launch (start us, length us, event | category | flops | bytes accessed | tf_op | source)
XLA Modules:
  0.0 164.5 jit_solution(7729399983581769809)
XLA Ops:
  8.0 2.4 %collective-permute-start = (f32[2,4,1,128]{3,1,2,0:T(4,128)S(1)}, f32[2,4,1,128]{3,1,2,0:T(4,128)S(1)}, u32[]{:S(2)}, u32[]{:S(2)}) collective-permute-start(f32[2,4,1,128]{3,1,2,0:T(4,128)S(1)} %pad_maximum_fusion.15), channel_id=1, source_target_pairs={{0,1},{2,3},{4,5},{6,7},{8,9},{10,11},{12,13},{14,15},{16,17},{18,... | collective-permute-start | bytes 12296 | tf_op jit(solution)/shard_map/ppermute | solution.py:32
  10.4 4.3 %collective-permute-start.1 = (f32[2,1,8,128]{3,1,2,0:T(1,128)S(1)}, f32[2,1,8,128]{3,1,2,0:T(1,128)S(1)}, u32[]{:S(2)}, u32[]{:S(2)}) collective-permute-start(f32[2,1,8,128]{3,1,2,0:T(1,128)S(1)} %pad_maximum_fusion.14), channel_id=1, source_target_pairs={{0,2},{2,4},{4,6},{1,3},{3,5},{5,7},{8,10},{10,12},{12,14},{9,11},... | collective-permute-start | bytes 24584 | tf_op jit(solution)/shard_map/ppermute | solution.py:32
  15.7 3.4 %collective-permute-start.10 = (f32[3,4,8,1]{3,2,1,0:T(8,128)S(1)}, f32[3,4,8,1]{3,2,1,0:T(8,128)S(1)}, u32[]{:S(2)}, u32[]{:S(2)}) collective-permute-start(f32[3,4,8,1]{3,2,1,0:T(8,128)S(1)} %get-tuple-element.92), channel_id=1, source_target_pairs={{0,8},{8,16},{16,24},{1,9},{9,17},{17,25},{2,10},{10,18},{18,26},{... | collective-permute-start | bytes 1160 | tf_op jit(solution)/shard_map/ppermute | solution.py:20
  19.1 1.3 collective-permute-start.11
  21.4 3.5 %collective-permute-start.2 = (f32[12,1,8,128]{3,1,2,0:T(1,128)S(1)}, f32[12,1,8,128]{3,1,2,0:T(1,128)S(1)}, u32[]{:S(2)}, u32[]{:S(2)}) collective-permute-start(f32[12,1,8,128]{3,1,2,0:T(1,128)S(1)} %get-tuple-element.66), channel_id=1, source_target_pairs={{0,2},{2,4},{4,6},{1,3},{3,5},{5,7},{8,10},{10,12},{12,14},{9,11},... | collective-permute-start | bytes 147464 | tf_op jit(solution)/shard_map/ppermute | solution.py:20
  32.2 3.5 %collective-permute-start.12 = (f32[3,1,8,34]{3,2,1,0:T(8,128)S(1)}, f32[3,1,8,34]{3,2,1,0:T(8,128)S(1)}, u32[]{:S(2)}, u32[]{:S(2)}) collective-permute-start(f32[3,1,8,34]{3,2,1,0:T(8,128)S(1)} %get-tuple-element.70), channel_id=1, source_target_pairs={{0,2},{2,4},{4,6},{1,3},{3,5},{5,7},{8,10},{10,12},{12,14},{9,11},... | collective-permute-start | bytes 9800 | tf_op jit(solution)/shard_map/ppermute | solution.py:20
  35.7 1.3 collective-permute-start.13
  37.1 4.2 %collective-permute-done.13 = f32[3,1,8,34]{3,2,1,0:T(8,128)S(1)} collective-permute-done((f32[3,1,8,34]{3,2,1,0:T(8,128)S(1)}, f32[3,1,8,34]{3,2,1,0:T(8,128)S(1)}, u32[]{:S(2)}, u32[]{:S(2)}) %collective-permute-start.13) | collective-permute-done | bytes 3296 | tf_op jit(solution)/shard_map/ppermute | solution.py:22
  41.5 1.4 collective-permute-start.14
  42.9 1.3 collective-permute-start.15
  47.0 4.5 %collective-permute-start.16 = (f32[3,4,8,1]{3,2,1,0:T(8,128)S(1)}, f32[3,4,8,1]{3,2,1,0:T(8,128)S(1)}, u32[]{:S(2)}, u32[]{:S(2)}) collective-permute-start(f32[3,4,8,1]{3,2,1,0:T(8,128)S(1)} %get-tuple-element.90), channel_id=1, source_target_pairs={{0,8},{8,16},{16,24},{1,9},{9,17},{17,25},{2,10},{10,18},{18,26},{... | collective-permute-start | bytes 1160 | tf_op jit(solution)/shard_map/ppermute | solution.py:20
  51.6 1.3 collective-permute-start.17
  53.5 4.8 %collective-permute-done.17 = f32[3,4,8,1]{3,2,1,0:T(8,128)S(1)} collective-permute-done((f32[3,4,8,1]{3,2,1,0:T(8,128)S(1)}, f32[3,4,8,1]{3,2,1,0:T(8,128)S(1)}, u32[]{:S(2)}, u32[]{:S(2)}) %collective-permute-start.17) | collective-permute-done | bytes 416 | tf_op jit(solution)/shard_map/ppermute | solution.py:22
  58.4 4.3 %collective-permute-start.18 = (f32[3,1,8,34]{3,2,1,0:T(8,128)S(1)}, f32[3,1,8,34]{3,2,1,0:T(8,128)S(1)}, u32[]{:S(2)}, u32[]{:S(2)}) collective-permute-start(f32[3,1,8,34]{3,2,1,0:T(8,128)S(1)} %get-tuple-element.68), channel_id=1, source_target_pairs={{0,2},{2,4},{4,6},{1,3},{3,5},{5,7},{8,10},{10,12},{12,14},{9,11},... | collective-permute-start | bytes 9800 | tf_op jit(solution)/shard_map/ppermute | solution.py:20
  63.9 18.1 %all-gather = f32[1,6,4,8,128]{3,2,1,0,4:T(4,128)S(1)} all-gather(f32[1,6,4,8,32]{3,2,1,0,4:T(4,128)S(1)} %copy.434), channel_id=2, replica_groups=mesh['grp'=4,'gx'=4,'gy'=2] {'grp'}, dimensions={4}, use_global_device_ids=true | all-gather | bytes 122880 | tf_op jit(solution)/shard_map/all_gather | solution.py:181
  85.5 1.7 %collective-permute-done.21 = f32[3,6,1,34]{3,1,2,0:T(8,128)S(1)} collective-permute-done((f32[3,6,1,34]{3,1,2,0:T(8,128)S(1)}, f32[3,6,1,34]{3,1,2,0:T(8,128)S(1)}, u32[]{:S(2)}, u32[]{:S(2)}) %collective-permute-start.21) | collective-permute-done | bytes 2480 | tf_op jit(solution)/shard_map/ppermute | solution.py:22
  87.5 2.1 %collective-permute-start.4 = (f32[12,6,1,128]{3,1,2,0:T(8,128)S(1)}, f32[12,6,1,128]{3,1,2,0:T(8,128)S(1)}, u32[]{:S(2)}, u32[]{:S(2)}) collective-permute-start(f32[12,6,1,128]{3,1,2,0:T(8,128)S(1)} %get-tuple-element.59), channel_id=1, source_target_pairs={{0,1},{2,3},{4,5},{6,7},{8,9},{10,11},{12,13},{14,15},{16,17},{18,... | collective-permute-start | bytes 110600 | tf_op jit(solution)/shard_map/ppermute | solution.py:20
  91.3 18.9 %all-gather.1 = f32[1,6,4,8,128]{3,2,1,0,4:T(4,128)S(1)} all-gather(f32[1,6,4,8,32]{3,2,1,0,4:T(4,128)S(1)} %copy.451), channel_id=3, replica_groups=mesh['grp'=4,'gx'=4,'gy'=2] {'grp'}, dimensions={4}, use_global_device_ids=true | all-gather | bytes 122880 | tf_op jit(solution)/shard_map/all_gather | solution.py:181
  114.3 4.2 %collective-permute-start.6 = (f32[12,1,8,128]{3,2,1,0:T(8,128)S(1)}, f32[12,1,8,128]{3,2,1,0:T(8,128)S(1)}, u32[]{:S(2)}, u32[]{:S(2)}) collective-permute-start(f32[12,1,8,128]{3,2,1,0:T(8,128)S(1)} %get-tuple-element.64), channel_id=1, source_target_pairs={{0,2},{2,4},{4,6},{1,3},{3,5},{5,7},{8,10},{10,12},{12,14},{9,11},... | collective-permute-start | bytes 147464 | tf_op jit(solution)/shard_map/ppermute | solution.py:20
  120.5 4.1 %collective-permute-done.7 = f32[12,1,8,128]{3,2,1,0:T(8,128)S(1)} collective-permute-done((f32[12,1,8,128]{3,2,1,0:T(8,128)S(1)}, f32[12,1,8,128]{3,2,1,0:T(8,128)S(1)}, u32[]{:S(2)}, u32[]{:S(2)}) %collective-permute-start.7) | collective-permute-done | bytes 49184 | tf_op jit(solution)/shard_map/ppermute | solution.py:22
  125.9 1.5 collective-permute-start.9
  127.4 1.6 collective-permute-done.9
  130.2 2.0 %copy_subtract_fusion.1 = (f32[4,3,5,9,129]{4,2,3,0,1:T(8,128)S(1)}, f32[4,3,5,9,129]{4,2,3,0,1:T(8,128)S(1)}, f32[4,3,5,9,129]{4,2,3,0,1:T(8,128)S(1)}) fusion(f32[4,3,5,9,129]{4,3,2,1,0:T(8,128)S(1)} %get-tuple-element.34, f32[4,3,5,9,129]{4,3,2,1,0:T(8,128)S(1)} %get-tuple-element.35, f32[4,3,5,9,129]{4,3,2,1,0:T(8,128)S(1)} %get-tuple-element.37, ...), kind=kLoop, calls=%fused_computation.16 | loop fusion | flops 208980 | bytes 1950480 | tf_op jit(solution)/shard_map/sub | solution.py:52
  136.3 19.7 %reduce-scatter.4.cloned.1.call-done = f32[32,64]{1,0:T(8,128)} async-done(((f32[128,64]{1,0:T(8,128)}), f32[32,64]{1,0:T(8,128)}) %reduce-scatter.4.cloned.1.call-update) | async-done | bytes 8208
  (156 shorter events, 32.7 us)
Async XLA Ops:
  7.2 148.9 %reduce-scatter.4.cloned.1.call-start = ((), (), s32[]{:S(2)}) async-start(), calls=%async_computation.1 | async-start | bytes 81920
  8.0 38.2 %collective-permute-start = (f32[2,4,1,128]{3,1,2,0:T(4,128)S(1)}, f32[2,4,1,128]{3,1,2,0:T(4,128)S(1)}, u32[]{:S(2)}, u32[]{:S(2)}) collective-permute-start(f32[2,4,1,128]{3,1,2,0:T(4,128)S(1)} %pad_maximum_fusion.15), channel_id=1, source_target_pairs={{0,1},{2,3},{4,5},{6,7},{8,9},{10,11},{12,13},{14,15},{16,17},{18,... | collective-permute-start | bytes 12296 | tf_op jit(solution)/shard_map/ppermute | solution.py:32
  10.4 35.8 %collective-permute-start.1 = (f32[2,1,8,128]{3,1,2,0:T(1,128)S(1)}, f32[2,1,8,128]{3,1,2,0:T(1,128)S(1)}, u32[]{:S(2)}, u32[]{:S(2)}) collective-permute-start(f32[2,1,8,128]{3,1,2,0:T(1,128)S(1)} %pad_maximum_fusion.14), channel_id=1, source_target_pairs={{0,2},{2,4},{4,6},{1,3},{3,5},{5,7},{8,10},{10,12},{12,14},{9,11},... | collective-permute-start | bytes 24584 | tf_op jit(solution)/shard_map/ppermute | solution.py:32
  15.7 16.5 %collective-permute-start.10 = (f32[3,4,8,1]{3,2,1,0:T(8,128)S(1)}, f32[3,4,8,1]{3,2,1,0:T(8,128)S(1)}, u32[]{:S(2)}, u32[]{:S(2)}) collective-permute-start(f32[3,4,8,1]{3,2,1,0:T(8,128)S(1)} %get-tuple-element.92), channel_id=1, source_target_pairs={{0,8},{8,16},{16,24},{1,9},{9,17},{17,25},{2,10},{10,18},{18,26},{... | collective-permute-start | bytes 1160 | tf_op jit(solution)/shard_map/ppermute | solution.py:20
  19.1 13.1 %collective-permute-start.11 = (f32[3,4,8,1]{3,2,1,0:T(8,128)S(1)}, f32[3,4,8,1]{3,2,1,0:T(8,128)S(1)}, u32[]{:S(2)}, u32[]{:S(2)}) collective-permute-start(f32[3,4,8,1]{3,2,1,0:T(8,128)S(1)} %get-tuple-element.93), channel_id=1, source_target_pairs={{8,0},{16,8},{24,16},{9,1},{17,9},{25,17},{10,2},{18,10},{26,18},{... | collective-permute-start | bytes 1160 | tf_op jit(solution)/shard_map/ppermute | solution.py:22
  21.4 66.0 %collective-permute-start.2 = (f32[12,1,8,128]{3,1,2,0:T(1,128)S(1)}, f32[12,1,8,128]{3,1,2,0:T(1,128)S(1)}, u32[]{:S(2)}, u32[]{:S(2)}) collective-permute-start(f32[12,1,8,128]{3,1,2,0:T(1,128)S(1)} %get-tuple-element.66), channel_id=1, source_target_pairs={{0,2},{2,4},{4,6},{1,3},{3,5},{5,7},{8,10},{10,12},{12,14},{9,11},... | collective-permute-start | bytes 147464 | tf_op jit(solution)/shard_map/ppermute | solution.py:20
  32.2 4.9 %collective-permute-start.12 = (f32[3,1,8,34]{3,2,1,0:T(8,128)S(1)}, f32[3,1,8,34]{3,2,1,0:T(8,128)S(1)}, u32[]{:S(2)}, u32[]{:S(2)}) collective-permute-start(f32[3,1,8,34]{3,2,1,0:T(8,128)S(1)} %get-tuple-element.70), channel_id=1, source_target_pairs={{0,2},{2,4},{4,6},{1,3},{3,5},{5,7},{8,10},{10,12},{12,14},{9,11},... | collective-permute-start | bytes 9800 | tf_op jit(solution)/shard_map/ppermute | solution.py:20
  35.7 5.6 %collective-permute-start.13 = (f32[3,1,8,34]{3,2,1,0:T(8,128)S(1)}, f32[3,1,8,34]{3,2,1,0:T(8,128)S(1)}, u32[]{:S(2)}, u32[]{:S(2)}) collective-permute-start(f32[3,1,8,34]{3,2,1,0:T(8,128)S(1)} %get-tuple-element.71), channel_id=1, source_target_pairs={{2,0},{4,2},{6,4},{3,1},{5,3},{7,5},{10,8},{12,10},{14,12},{11,9},... | collective-permute-start | bytes 9800 | tf_op jit(solution)/shard_map/ppermute | solution.py:22
  41.5 2.9 %collective-permute-start.14 = (f32[3,6,1,34]{3,1,2,0:T(8,128)S(1)}, f32[3,6,1,34]{3,1,2,0:T(8,128)S(1)}, u32[]{:S(2)}, u32[]{:S(2)}) collective-permute-start(f32[3,6,1,34]{3,1,2,0:T(8,128)S(1)} %get-tuple-element.80), channel_id=1, source_target_pairs={{0,1},{2,3},{4,5},{6,7},{8,9},{10,11},{12,13},{14,15},{16,17},{18,... | collective-permute-start | bytes 7352 | tf_op jit(solution)/shard_map/ppermute | solution.py:20
  42.9 3.1 %collective-permute-start.15 = (f32[3,6,1,34]{3,1,2,0:T(8,128)S(1)}, f32[3,6,1,34]{3,1,2,0:T(8,128)S(1)}, u32[]{:S(2)}, u32[]{:S(2)}) collective-permute-start(f32[3,6,1,34]{3,1,2,0:T(8,128)S(1)} %get-tuple-element.81), channel_id=1, source_target_pairs={{1,0},{3,2},{5,4},{7,6},{9,8},{11,10},{13,12},{15,14},{17,16},{19,... | collective-permute-start | bytes 7352 | tf_op jit(solution)/shard_map/ppermute | solution.py:22
  44.4 43.1 %collective-permute-start.3 = (f32[12,1,8,128]{3,1,2,0:T(1,128)S(1)}, f32[12,1,8,128]{3,1,2,0:T(1,128)S(1)}, u32[]{:S(2)}, u32[]{:S(2)}) collective-permute-start(f32[12,1,8,128]{3,1,2,0:T(1,128)S(1)} %get-tuple-element.67), channel_id=1, source_target_pairs={{2,0},{4,2},{6,4},{3,1},{5,3},{7,5},{10,8},{12,10},{14,12},{11,9},... | collective-permute-start | bytes 147464 | tf_op jit(solution)/shard_map/ppermute | solution.py:22
  47.0 6.5 %collective-permute-start.16 = (f32[3,4,8,1]{3,2,1,0:T(8,128)S(1)}, f32[3,4,8,1]{3,2,1,0:T(8,128)S(1)}, u32[]{:S(2)}, u32[]{:S(2)}) collective-permute-start(f32[3,4,8,1]{3,2,1,0:T(8,128)S(1)} %get-tuple-element.90), channel_id=1, source_target_pairs={{0,8},{8,16},{16,24},{1,9},{9,17},{17,25},{2,10},{10,18},{18,26},{... | collective-permute-start | bytes 1160 | tf_op jit(solution)/shard_map/ppermute | solution.py:20
  51.6 6.7 %collective-permute-start.17 = (f32[3,4,8,1]{3,2,1,0:T(8,128)S(1)}, f32[3,4,8,1]{3,2,1,0:T(8,128)S(1)}, u32[]{:S(2)}, u32[]{:S(2)}) collective-permute-start(f32[3,4,8,1]{3,2,1,0:T(8,128)S(1)} %get-tuple-element.91), channel_id=1, source_target_pairs={{8,0},{16,8},{24,16},{9,1},{17,9},{25,17},{10,2},{18,10},{26,18},{... | collective-permute-start | bytes 1160 | tf_op jit(solution)/shard_map/ppermute | solution.py:22
  58.4 24.3 %collective-permute-start.18 = (f32[3,1,8,34]{3,2,1,0:T(8,128)S(1)}, f32[3,1,8,34]{3,2,1,0:T(8,128)S(1)}, u32[]{:S(2)}, u32[]{:S(2)}) collective-permute-start(f32[3,1,8,34]{3,2,1,0:T(8,128)S(1)} %get-tuple-element.68), channel_id=1, source_target_pairs={{0,2},{2,4},{4,6},{1,3},{3,5},{5,7},{8,10},{10,12},{12,14},{9,11},... | collective-permute-start | bytes 9800 | tf_op jit(solution)/shard_map/ppermute | solution.py:20
  62.6 20.1 %collective-permute-start.19 = (f32[3,1,8,34]{3,2,1,0:T(8,128)S(1)}, f32[3,1,8,34]{3,2,1,0:T(8,128)S(1)}, u32[]{:S(2)}, u32[]{:S(2)}) collective-permute-start(f32[3,1,8,34]{3,2,1,0:T(8,128)S(1)} %get-tuple-element.69), channel_id=1, source_target_pairs={{2,0},{4,2},{6,4},{3,1},{5,3},{7,5},{10,8},{12,10},{14,12},{11,9},... | collective-permute-start | bytes 9800 | tf_op jit(solution)/shard_map/ppermute | solution.py:22
  82.7 44.6 %copy-start.2 = (f32[1,6,4,8,128]{4,2,3,1,0:T(4,128)}, f32[1,6,4,8,128]{4,2,3,1,0:T(4,128)S(1)}, u32[]{:S(2)}) copy-start(f32[1,6,4,8,128]{4,2,3,1,0:T(4,128)S(1)} %copy.435) | copy-start | bytes 294916
  82.9 2.6 %collective-permute-start.20 = (f32[3,6,1,34]{3,1,2,0:T(8,128)S(1)}, f32[3,6,1,34]{3,1,2,0:T(8,128)S(1)}, u32[]{:S(2)}, u32[]{:S(2)}) collective-permute-start(f32[3,6,1,34]{3,1,2,0:T(8,128)S(1)} %get-tuple-element.78), channel_id=1, source_target_pairs={{0,1},{2,3},{4,5},{6,7},{8,9},{10,11},{12,13},{14,15},{16,17},{18,... | collective-permute-start | bytes 7352 | tf_op jit(solution)/shard_map/ppermute | solution.py:20
  84.2 3.1 %collective-permute-start.21 = (f32[3,6,1,34]{3,1,2,0:T(8,128)S(1)}, f32[3,6,1,34]{3,1,2,0:T(8,128)S(1)}, u32[]{:S(2)}, u32[]{:S(2)}) collective-permute-start(f32[3,6,1,34]{3,1,2,0:T(8,128)S(1)} %get-tuple-element.79), channel_id=1, source_target_pairs={{1,0},{3,2},{5,4},{7,6},{9,8},{11,10},{13,12},{15,14},{17,16},{19,... | collective-permute-start | bytes 7352 | tf_op jit(solution)/shard_map/ppermute | solution.py:22
  87.5 24.0 %collective-permute-start.4 = (f32[12,6,1,128]{3,1,2,0:T(8,128)S(1)}, f32[12,6,1,128]{3,1,2,0:T(8,128)S(1)}, u32[]{:S(2)}, u32[]{:S(2)}) collective-permute-start(f32[12,6,1,128]{3,1,2,0:T(8,128)S(1)} %get-tuple-element.59), channel_id=1, source_target_pairs={{0,1},{2,3},{4,5},{6,7},{8,9},{10,11},{12,13},{14,15},{16,17},{18,... | collective-permute-start | bytes 110600 | tf_op jit(solution)/shard_map/ppermute | solution.py:20
  89.6 21.9 %collective-permute-start.5 = (f32[12,6,1,128]{3,1,2,0:T(8,128)S(1)}, f32[12,6,1,128]{3,1,2,0:T(8,128)S(1)}, u32[]{:S(2)}, u32[]{:S(2)}) collective-permute-start(f32[12,6,1,128]{3,1,2,0:T(8,128)S(1)} %get-tuple-element.60), channel_id=1, source_target_pairs={{1,0},{3,2},{5,4},{7,6},{9,8},{11,10},{13,12},{15,14},{17,16},{19,... | collective-permute-start | bytes 110600 | tf_op jit(solution)/shard_map/ppermute | solution.py:22
  114.3 6.1 %collective-permute-start.6 = (f32[12,1,8,128]{3,2,1,0:T(8,128)S(1)}, f32[12,1,8,128]{3,2,1,0:T(8,128)S(1)}, u32[]{:S(2)}, u32[]{:S(2)}) collective-permute-start(f32[12,1,8,128]{3,2,1,0:T(8,128)S(1)} %get-tuple-element.64), channel_id=1, source_target_pairs={{0,2},{2,4},{4,6},{1,3},{3,5},{5,7},{8,10},{10,12},{12,14},{9,11},... | collective-permute-start | bytes 147464 | tf_op jit(solution)/shard_map/ppermute | solution.py:20
  118.5 6.0 %collective-permute-start.7 = (f32[12,1,8,128]{3,2,1,0:T(8,128)S(1)}, f32[12,1,8,128]{3,2,1,0:T(8,128)S(1)}, u32[]{:S(2)}, u32[]{:S(2)}) collective-permute-start(f32[12,1,8,128]{3,2,1,0:T(8,128)S(1)} %get-tuple-element.65), channel_id=1, source_target_pairs={{2,0},{4,2},{6,4},{3,1},{5,3},{7,5},{10,8},{12,10},{14,12},{11,9},... | collective-permute-start | bytes 147464 | tf_op jit(solution)/shard_map/ppermute | solution.py:22
  124.6 2.8 %collective-permute-start.8 = (f32[12,6,1,128]{3,2,1,0:T(1,128)S(1)}, f32[12,6,1,128]{3,2,1,0:T(1,128)S(1)}, u32[]{:S(2)}, u32[]{:S(2)}) collective-permute-start(f32[12,6,1,128]{3,2,1,0:T(1,128)S(1)} %get-tuple-element.54), channel_id=1, source_target_pairs={{0,1},{2,3},{4,5},{6,7},{8,9},{10,11},{12,13},{14,15},{16,17},{18,... | collective-permute-start | bytes 110600 | tf_op jit(solution)/shard_map/ppermute | solution.py:20
  125.9 3.1 %collective-permute-start.9 = (f32[12,6,1,128]{3,2,1,0:T(1,128)S(1)}, f32[12,6,1,128]{3,2,1,0:T(1,128)S(1)}, u32[]{:S(2)}, u32[]{:S(2)}) collective-permute-start(f32[12,6,1,128]{3,2,1,0:T(1,128)S(1)} %get-tuple-element.55), channel_id=1, source_target_pairs={{1,0},{3,2},{5,4},{7,6},{9,8},{11,10},{13,12},{15,14},{17,16},{19,... | collective-permute-start | bytes 110600 | tf_op jit(solution)/shard_map/ppermute | solution.py:22
  (8 other events, 52.4 us)
Sparse Core Ops, SparseCore 0:
  135.1 20.9 reduce-scatter.3
where the time goes:
time: 166 us; the launch traced here: 164 us
  starting transfers between devices  49.3 us (30%)
  blocking collectives  37.1 us (22%)
  waiting for transfers between devices  36.8 us (22%)
  between operations  16.4 us (10%)
  other arithmetic  13.2 us (8%)
  local copies, waits for them, and re-layouts  11.7 us (7%)
    all_gather x2, blocking collectives, local(): master_whole = lax.all_gather(master_strain[0], 'grp', axis=3, tiled=True)  37.1 us
    ppermute x10, starting transfers between devices, with_halo(): lax.ppermute(tail, axis, [(i, (i + 1) % count) for i in range(ends)])  29.5 us
    unnamed x2, waiting for transfers between devices  19.8 us
    ppermute x10, waiting for transfers between devices, with_halo(): lax.ppermute(head, axis, [((i + 1) % count, i) for i in range(ends)])  16.7 us
    ppermute x10, starting transfers between devices, with_halo(): lax.ppermute(head, axis, [((i + 1) % count, i) for i in range(ends)])  13.1 us
    ppermute x2, starting transfers between devices, passed_along(): return lax.ppermute(value, axis, pairs)  6.67 us
    unnamed x36, local copies, waits for them, and re-layouts  5.5 us
  transfers between devices with their start and end apart: 23, of which 9 were waited for; matrix products, arithmetic and copies ran while one was open for 8% of the time, Pallas kernels for 0%

commit v1 on v0

v1 whole, which is shorter than its diff:
```python
import functools

import jax
import jax.numpy as jnp
from jax import lax
from jax.experimental import pallas as pl
from jax.experimental.pallas import tpu as pltpu
from jax.sharding import PartitionSpec as P

STEPS = 2
MESH = pl.DeviceIdType.MESH

time_step_sq = 0.0625


def kernel(
    sizes,
    master_cell,
    master_lag,
    master_trace,
    receiver_cell,
    receiver_lag,
    receiver_trace,
    fwd_now,
    fwd_prev,
    adj_now,
    adj_prev,
    lame_first,
    shear_mod,
    buoyancy,
    adj_out,
    kern_out,
    now,
    prev,
    mid,
    lame,
    shear,
    buoy,
    xlo,
    xhi,
    ylo,
    yhi,
    row_first,
    row_last,
    mod_send,
    mod_recv,
    low_stress,
    totals,
    share_send,
    share_recv,
    cells,
    amps,
    load_sem,
    send_sem,
    recv_sem,
):
    groups, count_x, count_y = sizes
    receivers, _, cells_x, cells_y, depth = adj_now.shape
    fields = receivers + 1
    grp = lax.axis_index("grp")
    gx = lax.axis_index("gx")
    gy = lax.axis_index("gy")
    has_down = gx > 0
    has_up = gx < count_x - 1
    has_left = gy > 0
    has_right = gy < count_y - 1
    corner_ul = jnp.logical_and(has_up, has_left)
    corner_dr = jnp.logical_and(has_down, has_right)
    down = (grp, gx - 1, gy)
    up = (grp, gx + 1, gy)
    left = (grp, gx, gy - 1)
    right = (grp, gx, gy + 1)
    up_left = (grp, gx + 1, gy - 1)
    down_right = (grp, gx - 1, gy + 1)
    peers = [(lax.rem(grp + d, groups), gx, gy) for d in range(1, groups)]
    sides = (
        (has_down, down),
        (has_up, up),
        (has_left, left),
        (has_right, right),
        (corner_ul, up_left),
        (corner_dr, down_right),
    )

    loads = [
        (adj_now, now.at[pl.ds(0, receivers)]),
        (fwd_now, now.at[receivers]),
        (lame_first, lame.at[pl.ds(1, cells_x)]),
        (shear_mod, shear.at[pl.ds(1, cells_x)]),
        (adj_prev, prev.at[pl.ds(0, receivers)]),
        (fwd_prev, prev.at[receivers]),
        (buoyancy, buoy),
    ]
    loads = [pltpu.make_async_copy(src, dst, load_sem.at[i]) for i, (src, dst) in enumerate(loads)]
    for copy in loads:
        copy.start()

    barrier = pltpu.get_barrier_semaphore()
    expected = jnp.int32(groups - 1)
    for there, where in sides:
        expected = expected + there.astype(jnp.int32)

        @pl.when(there)
        def _():
            pl.semaphore_signal(barrier, inc=1, device_id=where, device_id_type=MESH)

    for where in peers:
        pl.semaphore_signal(barrier, inc=1, device_id=where, device_id_type=MESH)

    for f in range(fields):
        master = f == receivers
        cells[f] = master_cell[0] if master else receiver_cell[f]
        lag = master_lag[0] if master else receiver_lag[f]
        for k in range(STEPS):
            for c in range(3):
                spot = (f * STEPS + k) * 3 + c
                amps[spot] = master_trace[c, lag + k] if master else receiver_trace[c, f, lag + k]

    @pl.when(jnp.logical_not(has_down))
    def _():
        xlo[...] = jnp.zeros_like(xlo)
        lame[0] = jnp.zeros_like(lame[0])
        shear[0] = jnp.zeros_like(shear[0])

    @pl.when(jnp.logical_not(has_up))
    def _():
        xhi[...] = jnp.zeros_like(xhi)

    @pl.when(jnp.logical_not(has_left))
    def _():
        ylo[:, :, 0:cells_x] = jnp.zeros_like(ylo[:, :, 0:cells_x])
        mod_recv[...] = jnp.zeros_like(mod_recv)

    @pl.when(jnp.logical_not(has_right))
    def _():
        yhi[:, :, 1 : cells_x + 1] = jnp.zeros_like(yhi[:, :, 1 : cells_x + 1])

    @pl.when(jnp.logical_not(corner_ul))
    def _():
        ylo[:, :, cells_x] = jnp.zeros_like(ylo[:, :, cells_x])

    @pl.when(jnp.logical_not(corner_dr))
    def _():
        yhi[:, :, 0] = jnp.zeros_like(yhi[:, :, 0])

    row_first[...] = jnp.zeros_like(row_first)
    row_last[...] = jnp.zeros_like(row_last)

    for copy in loads[:4]:
        copy.wait()

    def pack(f, carry):
        for c in range(3):
            for x in range(cells_x):
                row_first[0, c, x, pl.ds(f, 1), :] = now[f, c, x, 0:1, :]
                row_last[0, c, x, pl.ds(f, 1), :] = now[f, c, x, cells_y - 1 : cells_y, :]
        return carry

    lax.fori_loop(0, fields, pack, 0)
    for x in range(cells_x):
        mod_send[x : x + 1] = lame[x + 1, cells_y - 1 : cells_y, :]
        mod_send[cells_x + x : cells_x + x + 1] = shear[x + 1, cells_y - 1 : cells_y, :]

    pl.semaphore_wait(barrier, expected)

    number = [0]

    def remote(src, dst, where):
        i = number[0]
        number[0] += 1
        return pltpu.make_async_remote_copy(
            src_ref=src,
            dst_ref=dst,
            send_sem=send_sem.at[i],
            recv_sem=recv_sem.at[i],
            device_id=where,
            device_id_type=MESH,
        )

    def rows(k):
        return [
            (remote(row_first.at[k, :, cells_x - 1], yhi.at[k, :, 0], up_left), corner_ul, corner_dr),
            (remote(row_last.at[k, :, 0], ylo.at[k, :, cells_x], down_right), corner_dr, corner_ul),
            (remote(row_first.at[k], yhi.at[k, :, pl.ds(1, cells_x)], left), has_left, has_right),
            (remote(row_last.at[k], ylo.at[k, :, pl.ds(0, cells_x)], right), has_right, has_left),
        ]

    def start(copies):
        for copy, sends, _ in copies:
            pl.when(sends)(copy.start)

    def arrive(copies):
        for copy, _, gets in copies:
            pl.when(gets)(copy.wait_recv)

    def sent(copies):
        for copy, sends, _ in copies:
            pl.when(sends)(copy.wait_send)

    last = cells_x - 1
    group = pl.ds(0, receivers)
    first_round = [
        (remote(adj_now.at[:, :, 0], xhi.at[0, group], down), has_down, has_up),
        (remote(adj_now.at[:, :, last], xlo.at[0, group], up), has_up, has_down),
        (remote(fwd_now.at[:, 0], xhi.at[0, receivers], down), has_down, has_up),
        (remote(fwd_now.at[:, last], xlo.at[0, receivers], up), has_up, has_down),
        (remote(lame_first.at[last], lame.at[0], up), has_up, has_down),
        (remote(shear_mod.at[last], shear.at[0], up), has_up, has_down),
        (remote(mod_send, mod_recv, right), has_right, has_left),
    ] + rows(0)
    start(first_round)

    row_at = lax.broadcasted_iota(jnp.int32, (cells_y, depth), 0)
    lane_at = lax.broadcasted_iota(jnp.int32, (cells_y, depth), 1)
    flat_at = row_at * depth + lane_at
    top = row_at == 0
    bottom = row_at == cells_y - 1
    front = lane_at == 0
    back = lane_at == depth - 1
    plane_cells = cells_y * count_y * depth
    first_cell = gx * cells_x * plane_cells + gy * cells_y * depth

    def next_z(v):
        return jnp.where(back, 0.0, pltpu.roll(v, depth - 1, 1))

    def last_z(v):
        return jnp.where(front, 0.0, pltpu.roll(v, 1, 1))

    def next_y(v, row):
        return jnp.where(bottom, row, pltpu.roll(v, cells_y - 1, 0))

    def last_y(v, row):
        return jnp.where(top, row, pltpu.roll(v, 1, 0))

    def wall(k):
        for x in range(cells_x):
            here = [ylo[k, c, x] for c in range(3)]
            beside = [ylo[k, c, x + 1] for c in range(3)]
            above = [row_first[k, c, x] for c in range(3)]
            lam = mod_recv[x : x + 1]
            mu = mod_recv[cells_x + x : cells_x + x + 1]
            grad_y = [above[c] - here[c] for c in range(3)]
            xy = grad_y[0] + (beside[1] - here[1])
            yz = (next_z(here[1]) - here[1]) + grad_y[2]
            dilation = (beside[0] - here[0]) + grad_y[1] + (next_z(here[2]) - here[2])
            low_stress[k, 0, x] = mu * xy
            low_stress[k, 1, x] = lam * dilation + 2.0 * mu * grad_y[1]
            low_stress[k, 2, x] = mu * yz

    def step(k, f, state, earlier, put):
        one = pl.ds(f, 1)

        def row(c, x):
            return yhi[k, c, x + 1, one, :]

        here = [xlo[k, f, c] for c in range(3)]
        lam = lame[0]
        mu = shear[0]
        after = [state[f, c, 0] for c in range(3)]
        across = [next_y(here[c], row(c, -1)) for c in range(2)]
        along = [next_z(here[c]) for c in (0, 2)]
        xx = after[0] - here[0]
        dilation = xx + (across[1] - here[1]) + (along[1] - here[2])
        low = [
            lam * dilation + 2.0 * mu * xx,
            mu * ((across[0] - here[0]) + (after[1] - here[1])),
            mu * ((along[0] - here[0]) + (after[2] - here[2])),
        ]
        cell = cells[f]
        amp = [amps[(f * STEPS + k) * 3 + c] for c in range(3)]
        for x in range(cells_x):
            here = after
            after = [state[f, c, x + 1] if x < last else xhi[k, f, c] for c in range(3)]
            lam = lame[x + 1]
            mu = shear[x + 1]
            twice = 2.0 * mu
            gx_ = [after[c] - here[c] for c in range(3)]
            gy_ = [next_y(here[c], row(c, x)) - here[c] for c in range(3)]
            gz_ = [next_z(here[c]) - here[c] for c in range(3)]
            spread = lam * (gx_[0] + gy_[1] + gz_[2])
            xx = spread + twice * gx_[0]
            yy = spread + twice * gy_[1]
            zz = spread + twice * gz_[2]
            xy = mu * (gy_[0] + gx_[1])
            xz = mu * (gz_[0] + gx_[2])
            yz = mu * (gz_[1] + gy_[2])
            wall_xy, wall_yy, wall_yz = [low_stress[k, j, x, one, :] for j in range(3)]
            force = [
                (xx - low[0]) + (xy - last_y(xy, wall_xy)) + (xz - last_z(xz)),
                (xy - low[1]) + (yy - last_y(yy, wall_yy)) + (yz - last_z(yz)),
                (xz - low[2]) + (yz - last_y(yz, wall_yz)) + (zz - last_z(zz)),
            ]
            low = [xx, xy, xz]
            placed = flat_at == cell - (first_cell + x * plane_cells)
            scaled = time_step_sq * buoy[x]
            for c in range(3):
                moved = force[c] + jnp.where(placed, amp[c], 0.0)
                put(f, c, x, 2.0 * here[c] - earlier[f, c, x] + scaled * moved)

    def strain(planes, rows):
        for x in range(cells_x):
            here, after = planes[x], planes[x + 1]
            gx_ = [after[c] - here[c] for c in range(3)]
            gy_ = [next_y(here[c], rows[x][c]) - here[c] for c in range(3)]
            gz_ = [next_z(here[c]) - here[c] for c in range(3)]
            yield (
                gx_[0],
                gy_[1],
                gz_[2],
                gy_[0] + gx_[1],
                gz_[0] + gx_[2],
                gz_[1] + gy_[2],
            )

    def correlate(k, state):
        def summed(load):
            total = load(0)
            for f in range(1, receivers):
                total = total + load(f)
            return total

        whole, master = [], []
        for x in range(cells_x + 1):
            if x < cells_x:
                whole.append([summed(lambda f: state[f, c, x]) for c in range(3)])
                master.append([state[receivers, c, x] for c in range(3)])
            else:
                whole.append([summed(lambda f: xhi[k, f, c]) for c in range(3)])
                master.append([xhi[k, receivers, c] for c in range(3)])
        whole_rows = [
            [summed(lambda f: yhi[k, c, x + 1, f : f + 1, :]) for c in range(3)]
            for x in range(cells_x)
        ]
        master_rows = [
            [yhi[k, c, x + 1, receivers : receivers + 1, :] for c in range(3)]
            for x in range(cells_x)
        ]
        pairs = zip(strain(whole, whole_rows), strain(master, master_rows))
        for x, (a, b) in enumerate(pairs):
            swell = (a[0] + a[1] + a[2]) * (b[0] + b[1] + b[2])
            twist = 2.0 * (a[0] * b[0] + a[1] * b[1] + a[2] * b[2])
            twist = twist + (a[3] * b[3] + a[4] * b[4] + a[5] * b[5])
            if k == 0:
                totals[0, x] = swell
                totals[1, x] = twist
            else:
                totals[0, x] += swell
                totals[1, x] += twist

    for copy in loads[4:]:
        copy.wait()
    arrive(first_round)

    def put_mid(f, c, x, value):
        mid[f, c, x] = value
        row_first[1, c, x, pl.ds(f, 1), :] = value[0:1]
        row_last[1, c, x, pl.ds(f, 1), :] = value[cells_y - 1 : cells_y]

    def first_step(f, carry):
        step(0, f, now, prev, put_mid)
        return carry

    wall(0)
    lax.fori_loop(0, fields, first_step, 0)

    second_round = [
        (remote(mid.at[:, :, 0], xhi.at[1], down), has_down, has_up),
        (remote(mid.at[:, :, last], xlo.at[1], up), has_up, has_down),
    ] + rows(1)
    start(second_round)
    correlate(0, now)
    arrive(second_round)
    correlate(1, mid)

    share = depth // groups
    lane_part = lane_at // share
    for g in range(groups):
        for j in range(2):
            packed = None
            for x in range(cells_x):
                turn = (share * (x - g)) % depth
                piece = totals[j, x] if turn == 0 else pltpu.roll(totals[j, x], turn, 1)
                packed = piece if packed is None else jnp.where(lane_part == x, piece, packed)
            share_send[g, j] = packed
    third_round = [
        (remote(share_send.at[peers[d][0]], share_recv.at[d], peers[d]), True, True)
        for d in range(groups - 1)
    ]
    for copy, _, _ in third_round:
        copy.start()

    def put_out(f, c, x, value):
        adj_out[f, c, x] = value

    def last_step(f, carry):
        step(1, f, mid, now, put_out)
        return carry

    wall(1)
    lax.fori_loop(0, receivers, last_step, 0)

    for copy, _, _ in third_round:
        copy.wait_recv()
    scale_out = 1.0 / (STEPS * receivers * groups)
    for j in range(2):
        part = share_send[grp, j]
        for d in range(groups - 1):
            part = part + share_recv[d, j]
        part = part * scale_out
        for x in range(cells_x):
            piece = part if x == 0 else pltpu.roll(part, depth - share * x, 1)
            kern_out[j, x] = piece[:, 0:share]
    sent(first_round)
    sent(second_round)
    for copy, _, _ in third_round:
        copy.wait_send()


def local(
    fwd_now,
    fwd_prev,
    adj_now,
    adj_prev,
    lame_first,
    shear_mod,
    buoyancy,
    master_cell,
    master_lag,
    master_trace,
    receiver_cell,
    receiver_lag,
    receiver_trace,
):
    cells_x, cells_y, depth = lame_first.shape
    receivers = adj_now.shape[0]
    fields = receivers + 1
    sizes = tuple(lax.axis_size(axis) for axis in ("grp", "gx", "gy"))
    groups = sizes[0]
    lanes = -(-fields // 8) * 8
    block = (fields, 3, cells_x, cells_y, depth)
    scalars = pl.BlockSpec(memory_space=pltpu.SMEM)
    whole = pl.BlockSpec(memory_space=pl.ANY)
    vector = pl.BlockSpec(memory_space=pltpu.VMEM)

    def room(*shape):
        return pltpu.VMEM(shape, jnp.float32)

    return pl.pallas_call(
        functools.partial(kernel, sizes),
        out_shape=(
            jax.ShapeDtypeStruct(adj_now.shape, jnp.float32),
            jax.ShapeDtypeStruct((2, cells_x, cells_y, depth // groups), jnp.float32),
        ),
        in_specs=[scalars] * 6 + [whole] * 7,
        out_specs=(vector, vector),
        scratch_shapes=[
            room(*block),
            room(*block),
            room(*block),
            room(cells_x + 1, cells_y, depth),
            room(cells_x + 1, cells_y, depth),
            room(cells_x, cells_y, depth),
            room(STEPS, fields, 3, cells_y, depth),
            room(STEPS, fields, 3, cells_y, depth),
            room(STEPS, 3, cells_x + 1, lanes, depth),
            room(STEPS, 3, cells_x + 1, lanes, depth),
            room(STEPS, 3, cells_x, lanes, depth),
            room(STEPS, 3, cells_x, lanes, depth),
            room(2 * cells_x, depth),
            room(2 * cells_x, depth),
            room(STEPS, 3, cells_x, lanes, depth),
            room(2, cells_x, cells_y, depth),
            room(groups, 2, cells_y, depth),
            room(groups - 1, 2, cells_y, depth),
            pltpu.SMEM((fields,), jnp.int32),
            pltpu.SMEM((fields * STEPS * 3,), jnp.float32),
            pltpu.SemaphoreType.DMA((7,)),
            pltpu.SemaphoreType.DMA((32,)),
            pltpu.SemaphoreType.DMA((32,)),
        ],
        compiler_params=pltpu.CompilerParams(
            collective_id=0, has_side_effects=True, vmem_limit_bytes=56 * 1024 * 1024
        ),
    )(
        master_cell,
        master_lag,
        master_trace.T,
        receiver_cell,
        receiver_lag,
        receiver_trace.transpose(2, 0, 1),
        fwd_now,
        fwd_prev,
        adj_now,
        adj_prev,
        lame_first,
        shear_mod,
        buoyancy,
    )


def solution(mesh):
    in_specs = (
        P(None, "gx", "gy", None),
        P(None, "gx", "gy", None),
        P("grp", None, "gx", "gy", None),
        P("grp", None, "gx", "gy", None),
        P("gx", "gy", None),
        P("gx", "gy", None),
        P("gx", "gy", None),
        P(),
        P(),
        P(),
        P("grp"),
        P("grp"),
        P("grp", None, None),
    )
    out_specs = (P("grp", None, "gx", "gy", None), P(None, "gx", "gy", "grp"))
    return jax.shard_map(local, mesh=mesh, in_specs=in_specs, out_specs=out_specs, check_vma=False)
```

time: 166 us -> 23 us (0.14)
  starting transfers between devices: 49.3 us -> 0 us
  blocking collectives: 37.1 us -> 0 us
  waiting for transfers between devices: 36.8 us -> 0 us
  Pallas kernels: 0 us -> 18.6 us
  between operations: 16.4 us -> 1.94 us
  other arithmetic: 13.2 us -> 0 us
  local copies, waits for them, and re-layouts: 11.7 us -> 2.24 us
    ppermute x22 -> x0, starting transfers between devices: 49.2 us -> none  [the longest x10 29.5 us: with_halo(): lax.ppermute(tail, axis, [(i, (i + 1) % count) for i in range(ends)])]
    all_gather x2 -> x0, blocking collectives: 37.1 us -> none  [local(): master_whole = lax.all_gather(master_strain[0], 'grp', axis=3, tiled=True)]
    unnamed x2 -> x0, waiting for transfers between devices: 19.8 us -> none
    pallas_call x0 -> x1, Pallas kernels: none -> 18.6 us  [local(): pl.pallas_call(functools.partial(kernel, sizes), out_shape=(jax.ShapeDtyp...]
    ppermute x22 -> x0, waiting for transfers between devices: 17.1 us -> none  [the longest x10 16.7 us: with_halo(): lax.ppermute(head, axis, [((i + 1) % count, i) for i in range(ends)])]
    unnamed x36 -> x4, local copies, waits for them, and re-layouts: 5.5 us -> 2.24 us
    sub x5 -> x0, other arithmetic: 3.07 us -> none  [the longest x3 2.3 us: stencil(): grad_y = padded[:, :, :span_x + 1, 1:, :span_z + 1] - anchor]
    slice x13 -> x0, local copies, waits for them, and re-layouts: 2.49 us -> none  [the longest x6 1.13 us: with_halo(): lax.slice_in_dim(cells, cells.shape[dim] - width, cells.shape[dim], axis=...]
  transfers between devices with their start and end apart: 23 -> 0, of which waited for: 9 -> 0; matrix products, arithmetic and copies ran while one was open for 8% -> 0% of each run, Pallas kernels for 0% -> 0%
where the time goes in v1:
time: 23 us; the launch traced here: 22.7 us
  Pallas kernels  18.6 us (81%)
  local copies, waits for them, and re-layouts  2.24 us (10%)
  between operations  1.94 us (8%)
    pallas_call x1, Pallas kernels, local(): pl.pallas_call(functools.partial(kernel, sizes), out_shape=(jax.ShapeDtyp...  18.6 us
    unnamed x4, local copies, waits for them, and re-layouts  2.24 us

profile of v1, /device:TPU:0, one launch (start us, length us, event | category | flops | bytes accessed | tf_op | source)
XLA Modules:
  0.0 22.7 jit_solution(14353208890127516996)
XLA Ops:
  1.9 18.6 %shard_map.140 = (f32[4,3,4,8,128]{4,3,2,1,0:T(8,128)}, f32[2,4,8,32]{3,2,1,0:T(8,128)}) custom-call(s32[1]{0:T(128)S(6)} %copy.17.master_cell, s32[1]{0:T(128)S(6)} %copy.18.master_lag, f32[3,256]{1,0:T(4,128)} %bitcast.3, s32[4]{0:T(128)} %receiver_cell.1, s32[4]{0:T(128)} %receiver_lag.1, f32[3,4,256]{2,1,0:T(4,128)} %bitcast.2, ...), custom_call_target="tpu_custom_call" | custom-call | tf_op jit(solution)/shard_map/pallas_call | solution.py:448
  20.5 0.0 copy-start
  20.5 1.6 %copy.19 = f32[4,3,4,8,128]{4,3,2,1,0:T(8,128)} copy(f32[4,3,4,8,128]{4,3,2,1,0:T(8,128)} %get-tuple-element.4) | data formatting | bytes 393216
  22.1 0.0 copy-done
  22.1 0.6 %copy.20 = f32[2,4,8,32]{3,2,1,0:T(8,128)} copy(f32[2,4,8,32]{3,2,1,0:T(8,128)S(1)} %copy-done) | data formatting | bytes 16384
Async XLA Ops:
  20.5 1.6 %copy-start = (f32[2,4,8,32]{3,2,1,0:T(8,128)S(1)}, f32[2,4,8,32]{3,2,1,0:T(8,128)}, u32[]{:S(2)}) copy-start(f32[2,4,8,32]{3,2,1,0:T(8,128)} %get-tuple-element.5) | copy-start | bytes 24580
